TPU v7x, 128 devices: a whole 4x4x4 slice. The times are simulated.
128 devices in a mesh: space: 8 (over x_hi, z), vel: 16 (over y, x_lo, core).
Axes of the slice: x: 4 (x_hi: 2, x_lo: 2; x = x_hi * 2 + x_lo), y: 4, z: 4, core: 2. Of those that a mesh axis runs over, the one named last changes fastest.
Arguments:
- distribution: float32 [512, 32768], P('space', 'vel'), may hold values from 0.3 to 3
- wall_flags: int32 [512], P('space'), may hold values from 0 to 1, as said below
- cell_slab: int32 [512], P('space'), may hold values from 0 to 15
- species: int32 [512], P('space'), may hold values from 0 to 1
- normal_kernel: float32 [2, 32, 32], replicated, may hold values from 0 to 1, as said below
- tangent_kernel: float32 [2, 32, 32], replicated, may hold values from 0 to 1, as said below
- blow_rate: float32 [16], replicated, may hold values from 0.2 to 2
- emitted: float32 [32768], replicated, may hold values from 0.2 to 2
- spectral: float32 [5, 32768], replicated, may hold values from 0.05 to 1
- collide_rate: float32 [2], replicated, may hold values from 0.3 to 1
Outputs:
- updated: float32 [512, 32768], P('space', 'vel')
Inputs may be any that keep to these rules, and one draw needn't show every extreme that they name: `wall_flags`: in each row of 32 cells along the wall normal exactly one cell is flagged, at a normal index below 4. `normal_kernel`: entries are positive. `tangent_kernel`: entries are positive.
All inputs are finite; a program needn't handle non-finite values.
Results may differ from a plain program's by a relative error of at most 0.0003.
Values sent between devices are 32-bit elements; how exact they have to be, the bound alone decides.
A program may use at most 128 MiB of HBM per device.

v0:
```python
import functools

import jax
import jax.numpy as jnp
import ml_dtypes
import numpy as np
from jax import lax
from jax.experimental import pallas as pl
from jax.experimental.pallas import tpu as pltpu
from jax.sharding import PartitionSpec as P

NV = 32
GX = 32
Q = NV * NV
HALF = Q // 2
OWN = 4
VEL = 16
SPACE = 8
ROWS = NV * OWN
FACTORS = 5
PAIRS = 2
courant = 0.12
top_speed = 4.0
collide_step = 0.5
MESH = pl.DeviceIdType.MESH
f32 = jnp.float32
bf16 = jnp.bfloat16


def parts_of(table):
    hi = table.astype(np.float32).astype(ml_dtypes.bfloat16)
    lo = (table - hi.astype(np.float64)).astype(np.float32).astype(ml_dtypes.bfloat16)
    return hi, lo


def class_slots(parity):
    seen, slots = set(), []
    for kj in range(parity, NV, 2):
        for kl in range(NV):
            other = ((-kj) % NV, (-kl) % NV)
            if other == (kj, kl) or (kj, kl) in seen:
                continue
            seen.add((kj, kl))
            seen.add(other)
            slots.append((kj, kl))
    return slots


def tables():
    j, l = np.divmod(np.arange(HALF), NV)

    def angle(k):
        return 2 * np.pi * ((k[0] * j + k[1] * l) % NV) / NV

    selfs = [((0, 0), (16, 0)), ((0, 16), (16, 16))]
    even, odd = class_slots(0), class_slots(1)
    pair = np.sqrt(2.0) / NV
    t_even = np.zeros((HALF, HALF))
    t_odd = np.zeros((HALF, HALF))
    quarter = HALF // 2
    for n, (a, b) in enumerate(selfs):
        t_even[:, n] = np.cos(angle(a)) / NV
        t_even[:, quarter + n] = np.cos(angle(b)) / NV
    for n, k in enumerate(even):
        t_even[:, n + 2] = pair * np.cos(angle(k))
        t_even[:, quarter + n + 2] = -pair * np.sin(angle(k))
    for n, k in enumerate(odd):
        t_odd[:, n] = pair * np.cos(angle(k))
        t_odd[:, quarter + n] = -pair * np.sin(angle(k))
    big = np.stack(parts_of(t_even) + parts_of(t_odd) + parts_of(t_even.T) + parts_of(t_odd.T))

    phase = 2 * np.pi * (np.outer(np.arange(NV), np.arange(NV)) % NV) / NV
    c = np.kron(np.cos(phase), np.eye(OWN))
    s = np.kron(np.sin(phase), np.eye(OWN))
    fwd = np.block([[c, s], [-s, c]])
    flip = np.block([[c, -s], [-s, -c]])
    inv = np.block([[c, -s], [s, c]])
    left = np.stack(parts_of(fwd) + parts_of(flip) + parts_of(inv))

    w = 0.5 / NV
    width = HALF + 128
    pick = np.zeros((2, Q, width))

    def put(column, k, weight):
        pick[0, k[0] * NV + k[1], column] += weight
        pick[1, ((-k[0]) % NV) * NV + ((-k[1]) % NV), column] += weight

    for n, (a, b) in enumerate(selfs):
        put(n, a, w / 2)
        put(n, b, w / 2)
        put(HALF + n, a, w / 2)
        put(HALF + n, b, -w / 2)
    for n, k in enumerate(even):
        put(n + 2, k, w)
    for n, k in enumerate(odd):
        put(quarter + n, k, w)
    pick = np.concatenate([pick[0], pick[1]], axis=1).astype(ml_dtypes.bfloat16)

    row = np.kron(np.eye(NV), np.ones((OWN, 1)))
    back_row = row[:, (-np.arange(NV)) % NV]
    spread = np.concatenate([row, back_row], axis=1).astype(ml_dtypes.bfloat16)
    row_j = np.kron(np.eye(NV), np.ones((1, NV))).astype(ml_dtypes.bfloat16)
    row_l = np.kron(np.ones((1, NV)), np.eye(NV)).astype(ml_dtypes.bfloat16)
    return big, left, pick, spread, row.astype(ml_dtypes.bfloat16), np.ascontiguousarray(row.T).astype(
        ml_dtypes.bfloat16
    ), np.stack([row_j, row_l])


def split(x):
    hi = x.astype(bf16)
    return hi, (x - hi.astype(f32)).astype(bf16)


def dot(a, b):
    return jnp.dot(a, b, preferred_element_type=f32)


def dot3(x, y):
    return dot(x[0], y[0]) + (dot(x[1], y[0]) + dot(x[0], y[1]))


def kernel(
    x_hbm,
    spectral_hbm,
    big_hbm,
    pick_hbm,
    left,
    spread,
    row_out,
    row_in,
    lanes_in,
    normal,
    tangent,
    emitted,
    flags,
    slabs,
    species,
    blow,
    rates,
    back,
    xv,
    upper,
    lower,
    send,
    recv,
    result,
    big,
    pick,
    spec,
    spec_rows,
    weights,
    weights_self,
    wall_hi,
    wall_lo,
    grid_hi,
    grid_lo,
    local_sem,
    halo_send,
    halo_recv,
    out_send,
    out_recv,
    back_send,
    back_recv,
):
    space = lax.axis_index("space")
    vel = lax.axis_index("vel")
    place_y, place_x, place_c = vel // 4, (vel // 2) % 2, vel % 2
    after, before = (space + 1) % SPACE, (space + SPACE - 1) % SPACE

    def peer(dy, dx, dc):
        return ((place_y + dy) % 4) * 4 + ((place_x + dx) % 2) * 2 + (place_c + dc) % 2

    offsets = [
        (dy, dx, dc)
        for dy in (2, 1, 3, 0)
        for dx in (1, 0)
        for dc in (1, 0)
        if (dy, dx, dc) != (0, 0, 0)
    ]

    load_x = pltpu.make_async_copy(x_hbm, xv, local_sem.at[0])
    load_spec = pltpu.make_async_copy(spectral_hbm, spec, local_sem.at[1])
    load_pick = pltpu.make_async_copy(pick_hbm, pick, local_sem.at[2])
    load_big = pltpu.make_async_copy(big_hbm, big, local_sem.at[3])
    load_x.start()
    load_spec.start()
    load_pick.start()
    load_big.start()

    barrier = pltpu.get_barrier_semaphore()
    for step in range(1, VEL):
        pl.semaphore_signal(
            barrier, inc=1, device_id=(space, (vel + step) % VEL), device_id_type=MESH
        )
    for other in (after, before):
        pl.semaphore_signal(barrier, inc=1, device_id=(other, vel), device_id_type=MESH)
    pl.semaphore_wait(barrier, VEL + 1)

    halos = []
    for own in range(2):
        low = pl.ds(own * Q, HALF)
        high = pl.ds(own * Q + HALF, HALF)
        for number, (src, dst, other) in enumerate(
            (
                (x_hbm.at[pl.ds(0, GX), low], upper, before),
                (x_hbm.at[pl.ds(GX, GX), high], lower, after),
            )
        ):
            copy = pltpu.make_async_remote_copy(
                src_ref=src,
                dst_ref=dst.at[own],
                send_sem=halo_send.at[number, own],
                recv_sem=halo_recv.at[number, own],
                device_id=(other, vel),
                device_id_type=MESH,
            )
            copy.start()
            halos.append(copy)
    load_x.wait()

    lane = lax.broadcasted_iota(jnp.int32, (1, HALF), 1)
    cell = lax.broadcasted_iota(jnp.int32, (GX, HALF), 0)
    sub = lax.broadcasted_iota(jnp.int32, (GX // 8, 8, HALF), 1)

    def speed(index):
        return courant * ((2.0 * index.astype(f32) + 1.0 - NV) / NV * top_speed)

    def upwind(group, half, own, neighbour):
        at = own * Q + half * HALF
        f = xv[group * GX : (group + 1) * GX, at : at + HALF]
        wall_side = jnp.where(cell == 0, 0.0, pltpu.roll(f, 1, 0))
        far_side = jnp.where(cell == GX - 1, 0.0, pltpu.roll(f, GX - 1, 0))
        a = speed(vel * 2 + own)
        b = speed((lane + half * HALF) // NV)
        read = f - jnp.maximum(a, 0.0) * (f - wall_side)
        read = read - jnp.minimum(a, 0.0) * (far_side - f)
        return read - jnp.abs(b) * (f - neighbour)

    def pack(group, half, neighbours):
        r0, r1 = (
            upwind(group, half, own, neighbours[own]).reshape(GX // 8, 8, HALF) for own in range(2)
        )
        first = jnp.where(sub < 4, r0, pltpu.roll(r1, 4, 1))
        second = jnp.where(sub < 4, pltpu.roll(r0, 4, 1), r1)
        lanes = slice(half * HALF, (half + 1) * HALF)
        for m in range(GX // 8):
            send[8 * group + 2 * m, :, lanes] = first[m]
            send[8 * group + 2 * m + 1, :, lanes] = second[m]

    def piece(phase, number, owner, dest):
        half = (dest // 8 + phase) % 2
        lanes = pl.ds(pl.multiple_of(half * HALF, HALF), HALF)
        return pltpu.make_async_remote_copy(
            src_ref=send.at[dest, :, lanes],
            dst_ref=recv.at[owner, :, lanes],
            send_sem=out_send.at[phase, number],
            recv_sem=out_recv.at[phase, owner],
            device_id=(space, dest),
            device_id_type=MESH,
        )

    def send_phase(phase):
        for number, offset in enumerate(offsets):
            piece(phase, number, vel, peer(*offset)).start()

    for group in range(2):
        half = group
        at = half * HALF
        other = slice((1 - group) * GX, (2 - group) * GX)
        pack(group, half, [xv[other, own * Q + at : own * Q + at + HALF] for own in range(2)])
    send_phase(0)

    for copy in halos:
        copy.wait_recv()
    pack(0, 1, [lower[own] for own in range(2)])
    pack(1, 0, [upper[own] for own in range(2)])
    send_phase(1)
    keep = pltpu.make_async_copy(send.at[vel], recv.at[vel], local_sem.at[0])
    keep.start()

    load_spec.wait()
    zero3 = jnp.zeros((8 - FACTORS, Q), f32)
    for k in range(NV):
        spec_rows[k] = jnp.concatenate([spec[:, k * Q : (k + 1) * Q], zero3], axis=0)
    load_pick.wait()
    width = HALF + 128
    for r in range(FACTORS):
        row_hi, row_lo = split(spec_rows[:, r, :])
        both = dot(row_hi, pick[...]) + dot(row_lo, pick[...])
        both = jnp.concatenate([both[:, :width], both[:, width:]], axis=0)
        both_hi, both_lo = split(both)
        whole = dot(spread[...], both_hi) + dot(spread[...], both_lo)
        weights[r] = whole[:, :HALF]
        weights_self[r] = whole[:, HALF:]

    row_id = lax.broadcasted_iota(jnp.int32, (ROWS, 1), 0) % OWN
    first_cell = vel * OWN
    rate_column = jnp.zeros((ROWS, 1), f32)
    for c in range(OWN):
        rate = jnp.where(species[first_cell + c] == 1, rates[1], rates[0])
        rate_column = jnp.where(row_id == c, collide_step * rate, rate_column)

    wall_here = vel % 8 == 0
    kind = 0
    slab = 0
    for c in range(OWN):
        kind = kind + flags[first_cell + c] * species[first_cell + c]
        slab = slab + flags[first_cell + c] * slabs[first_cell + c]

    @pl.when(wall_here)
    def _():
        turn = split(jnp.where(kind == 1, tangent[1], tangent[0]))
        by_j = dot(turn[0], lanes_in[0]) + dot(turn[1], lanes_in[0])
        by_l = dot(turn[0], lanes_in[1]) + dot(turn[1], lanes_in[1])
        for j in range(NV):
            hi, lo = split(by_j[j : j + 1, :] * by_l)
            wall_hi[j * NV : (j + 1) * NV, :] = hi
            wall_lo[j * NV : (j + 1) * NV, :] = lo

    for phase in range(2):
        for offset in offsets:
            piece(phase, 0, peer(*offset), vel).wait_recv()
    keep.wait()

    @pl.when(wall_here)
    def _():
        scatter = split(jnp.where(kind == 1, normal[1], normal[0]))
        wide = split(dot(row_out[...], scatter[0]) + dot(row_out[...], scatter[1]))
        wide = dot(wide[0], row_in[...]) + dot(wide[1], row_in[...])
        same = row_id == lax.broadcasted_iota(jnp.int32, (1, ROWS), 1) % OWN
        wide = split(jnp.where(same, wide, 0.0))
        x = recv[...].reshape(ROWS, Q)
        turned = split(dot3(split(x), (wall_hi[...], wall_lo[...])))
        reflected = dot3(wide, turned)
        gas = jnp.concatenate(
            [emitted[pl.ds(t, NV, stride=Q // 128), :] for t in range(Q // 128)], axis=1
        )
        gas = split(gas)
        gas = dot(row_out[...], gas[0]) + dot(row_out[...], gas[1])
        reflected = reflected + blow[slab] * gas
        flag_column = jnp.zeros((ROWS, 1), jnp.int32)
        for c in range(OWN):
            flag_column = jnp.where(row_id == c, flags[first_cell + c], flag_column)
        recv[...] = jnp.where(flag_column == 1, reflected, x).reshape(VEL, 8, Q)

    load_big.wait()
    quarter = HALF // 2
    xa = recv[:, :, :HALF].reshape(ROWS, HALF)
    xb = recv[:, :, HALF:].reshape(ROWS, HALF)
    ye = dot3(split(xa + xb), (big[0], big[1]))
    yo = dot3(split(xa - xb), (big[2], big[3]))
    z = jnp.concatenate(
        [
            jnp.concatenate([ye[:, :quarter], yo[:, :quarter]], axis=1),
            jnp.concatenate([ye[:, quarter:], yo[:, quarter:]], axis=1),
        ],
        axis=0,
    )
    z = split(z)
    spectrum = dot3((left[0], left[1]), z)
    mirrored = dot3((left[2], left[3]), (z[0][:, :128], z[1][:, :128]))
    for r in range(FACTORS):
        w = jnp.concatenate([weights[r], weights[r]], axis=0)
        d = jnp.concatenate([weights_self[r], weights_self[r]], axis=0)
        scaled = spectrum * w
        first = scaled[:, :128] + mirrored * d
        scaled = split(jnp.concatenate([first, scaled[:, 128:]], axis=1))
        hi, lo = split(dot3((left[4], left[5]), scaled))
        for part, grid in ((hi, grid_hi), (lo, grid_lo)):
            for block in range(2):
                lanes = slice(block * quarter, (block + 1) * quarter)
                grid[block, r, :, :quarter] = part[:ROWS, lanes]
                grid[block, r, :, quarter:] = part[ROWS:, lanes]

    def home(number, dest):
        return pltpu.make_async_remote_copy(
            src_ref=result.at[dest],
            dst_ref=back.at[vel],
            send_sem=back_send.at[number],
            recv_sem=back_recv.at[vel],
            device_id=(space, dest),
            device_id_type=MESH,
        )

    def arrival(owner):
        return pltpu.make_async_remote_copy(
            src_ref=result.at[vel],
            dst_ref=back.at[owner],
            send_sem=back_send.at[0],
            recv_sem=back_recv.at[owner],
            device_id=(space, owner),
            device_id_type=MESH,
        )

    count = ROWS // 4
    rate_part = rate_column[:count]
    for dy in (2, 1, 3, 0):
        plane = (place_y + dy) % 4
        rows = pl.ds(pl.multiple_of(plane * count, count), count)
        sums = []
        for block in range(2):
            lhs = [
                jnp.concatenate([grid[block, r, rows, :] for r in range(FACTORS)], axis=0)
                for grid in (grid_hi, grid_lo)
            ]
            sums.append(dot3(lhs, (big[4 + 2 * block], big[5 + 2 * block])))
        planes = pl.ds(plane * 4, 4)
        for half, total in ((0, sums[0] + sums[1]), (1, sums[0] - sums[1])):
            filtered = [total[r * count : (r + 1) * count] for r in range(FACTORS)]
            walled = recv[planes, :, half * HALF : (half + 1) * HALF].reshape(count, HALF)
            gained = filtered[0] * filtered[2] + filtered[1] * filtered[3]
            updated = walled + rate_part * (gained - walled * filtered[4])
            result[planes, :, half * HALF : (half + 1) * HALF] = updated.reshape(4, 8, HALF)
        for number, offset in enumerate(offsets):
            if offset[0] == dy:
                home(number, peer(*offset)).start()
    keep = pltpu.make_async_copy(result.at[vel], back.at[vel], local_sem.at[0])
    keep.start()

    for copy in halos:
        copy.wait_send()
    for number, offset in enumerate(offsets):
        for phase in range(2):
            piece(phase, number, vel, peer(*offset)).wait_send()
        home(number, peer(*offset)).wait_send()
        arrival(peer(*offset)).wait_recv()
    keep.wait()


def unpack(back, out):
    for m in range(GX // 4):
        first, second = back[2 * m], back[2 * m + 1]
        sub = lax.broadcasted_iota(jnp.int32, (8, Q), 0)
        out[8 * m : 8 * m + 8, :Q] = jnp.where(sub < 4, first, pltpu.roll(second, 4, 0))
        out[8 * m : 8 * m + 8, Q:] = jnp.where(sub < 4, pltpu.roll(first, 4, 0), second)


def on_device(
    distribution,
    wall_flags,
    cell_slab,
    species,
    normal_kernel,
    tangent_kernel,
    blow_rate,
    emitted,
    spectral,
    collide_rate,
):
    big, left, pick, spread, row_out, row_in, lanes_in = tables()
    anywhere = pl.BlockSpec(memory_space=pl.ANY)
    vmem = pl.BlockSpec(memory_space=pltpu.VMEM)
    smem = pl.BlockSpec(memory_space=pltpu.SMEM)
    width = HALF + 128
    dma = pltpu.SemaphoreType.DMA
    back = pl.pallas_call(
        kernel,
        out_shape=jax.ShapeDtypeStruct((VEL, 8, Q), f32),
        in_specs=[anywhere] * 4 + [vmem] * 8 + [smem] * 5,
        out_specs=vmem,
        scratch_shapes=[
            pltpu.VMEM((2 * GX, 2 * Q), f32),
            pltpu.VMEM((2, GX, HALF), f32),
            pltpu.VMEM((2, GX, HALF), f32),
            pltpu.VMEM((VEL, 8, Q), f32),
            pltpu.VMEM((VEL, 8, Q), f32),
            pltpu.VMEM((VEL, 8, Q), f32),
            pltpu.VMEM((8, HALF, HALF), bf16),
            pltpu.VMEM((Q, 2 * width), bf16),
            pltpu.VMEM((FACTORS, NV * Q), f32),
            pltpu.VMEM((NV, 8, Q), f32),
            pltpu.VMEM((FACTORS, ROWS, HALF), f32),
            pltpu.VMEM((FACTORS, ROWS, 128), f32),
            pltpu.VMEM((Q, Q), bf16),
            pltpu.VMEM((Q, Q), bf16),
            pltpu.VMEM((2, FACTORS, ROWS, HALF), bf16),
            pltpu.VMEM((2, FACTORS, ROWS, HALF), bf16),
            dma((4,)),
            dma((2, 2)),
            dma((2, 2)),
            dma((2, VEL)),
            dma((2, VEL)),
            dma((VEL,)),
            dma((VEL,)),
        ],
        compiler_params=pltpu.CompilerParams(
            collective_id=0, has_side_effects=True, vmem_limit_bytes=48 * 2**20
        ),
        name="step",
    )(
        distribution,
        spectral,
        jnp.asarray(big),
        jnp.asarray(pick),
        jnp.asarray(left),
        jnp.asarray(spread),
        jnp.asarray(row_out),
        jnp.asarray(row_in),
        jnp.asarray(lanes_in),
        normal_kernel,
        jnp.swapaxes(tangent_kernel, 1, 2),
        emitted.reshape(NV * Q // 128, 128),
        wall_flags,
        cell_slab,
        species,
        blow_rate,
        collide_rate,
    )
    return pl.pallas_call(
        unpack,
        out_shape=jax.ShapeDtypeStruct((2 * GX, 2 * Q), f32),
        in_specs=[vmem],
        out_specs=vmem,
        name="unpack",
    )(back)


def solution(mesh):
    in_specs = (P("space", "vel"), P("space"), P("space"), P("space"), P(), P(), P(), P(), P(), P())
    out_specs = P("space", "vel")
    return jax.shard_map(
        on_device, mesh=mesh, in_specs=in_specs, out_specs=out_specs, check_vma=False
    )
```

profile of v0, /device:TPU:1, one launch (start us, length us, event | category | flops | bytes accessed | tf_op | source)
XLA Modules:
  0.0 51.1 jit_solution(11476230314874719759)
XLA Ops:
  0.0 0.8 %copy.18 = f32[2,32,32]{1,2,0:T(8,128)S(1)} copy(f32[2,32,32]{2,1,0:T(8,128)} %param.22) | data formatting | bytes 16384 | tf_op args[5]
  0.8 0.0 copy-start
  0.8 1.7 %copy-done = bf16[1024,1280]{1,0:T(8,128)(2,1)S(1)} copy-done((bf16[1024,1280]{1,0:T(8,128)(2,1)S(1)}, bf16[1024,1280]{1,0:T(8,128)(2,1)}, u32[]{:S(2)}) %copy-start) | copy-done | bytes 2621464
  2.6 0.0 copy-start.2
  2.6 1.2 %copy-done.2 = f32[5,32768]{1,0:T(8,128)S(1)} copy-done((f32[5,32768]{1,0:T(8,128)S(1)}, f32[5,32768]{1,0:T(8,128)}, u32[]{:S(2)}) %copy-start.2) | copy-done | bytes 655384
  3.8 0.0 copy-start.3
  3.8 1.1 %copy-done.3 = bf16[6,256,256]{2,1,0:T(8,128)(2,1)S(1)} copy-done((bf16[6,256,256]{2,1,0:T(8,128)(2,1)S(1)}, bf16[6,256,256]{2,1,0:T(8,128)(2,1)}, u32[]{:S(2)}) %copy-start.3) | copy-done | bytes 786456
  4.9 0.0 copy-start.4
  4.9 1.0 %copy-done.4 = f32[64,2048]{1,0:T(8,128)S(1)} copy-done((f32[64,2048]{1,0:T(8,128)S(1)}, f32[64,2048]{1,0:T(8,128)}, u32[]{:S(2)}) %copy-start.4) | copy-done | bytes 524312
  6.0 0.9 %copy-done.5 = f32[32768]{0:T(1024)S(1)} copy-done((f32[32768]{0:T(1024)S(1)}, f32[32768]{0:T(1024)}, u32[]{:S(2)}) %copy-start.5) | copy-done | bytes 131096
  6.9 0.9 %copy-done.6 = bf16[2,32,1024]{2,1,0:T(8,128)(2,1)S(1)} copy-done((bf16[2,32,1024]{2,1,0:T(8,128)(2,1)S(1)}, bf16[2,32,1024]{2,1,0:T(8,128)(2,1)}, u32[]{:S(2)}) %copy-start.6) | copy-done | bytes 131096
  7.8 0.8 %copy-done.7 = f32[2,32,32]{2,1,0:T(8,128)S(1)} copy-done((f32[2,32,32]{2,1,0:T(8,128)S(1)}, f32[2,32,32]{2,1,0:T(8,128)}, u32[]{:S(2)}) %copy-start.7) | copy-done | bytes 8216
  8.5 0.8 %copy-done.8 = bf16[128,32]{1,0:T(8,128)(2,1)S(1)} copy-done((bf16[128,32]{1,0:T(8,128)(2,1)S(1)}, bf16[128,32]{1,0:T(8,128)(2,1)}, u32[]{:S(2)}) %copy-start.8) | copy-done | bytes 8216
  9.3 0.8 %copy-done.9 = bf16[128,64]{1,0:T(8,128)(2,1)S(1)} copy-done((bf16[128,64]{1,0:T(8,128)(2,1)S(1)}, bf16[128,64]{1,0:T(8,128)(2,1)}, u32[]{:S(2)}) %copy-start.9) | copy-done | bytes 16408
  10.1 0.7 %copy-done.10 = bf16[32,128]{1,0:T(8,128)(2,1)S(1)} copy-done((bf16[32,128]{1,0:T(8,128)(2,1)S(1)}, bf16[32,128]{1,0:T(8,128)(2,1)}, u32[]{:S(2)}) %copy-start.10) | copy-done | bytes 8216
  10.8 0.7 %copy-done.11 = s32[64]{0:T(128)S(1)} copy-done((s32[64]{0:T(128)S(1)}, s32[64]{0:T(128)}, u32[]{:S(2)}) %copy-start.11) | copy-done | bytes 280
  11.4 0.7 %copy-done.12 = s32[64]{0:T(128)S(1)} copy-done((s32[64]{0:T(128)S(1)}, s32[64]{0:T(128)}, u32[]{:S(2)}) %copy-start.12) | copy-done | bytes 280
  12.1 0.7 %copy-done.13 = s32[64]{0:T(128)S(1)} copy-done((s32[64]{0:T(128)S(1)}, s32[64]{0:T(128)}, u32[]{:S(2)}) %copy-start.13) | copy-done | bytes 280
  12.7 0.7 %copy-done.14 = f32[16]{0:T(128)S(1)} copy-done((f32[16]{0:T(128)S(1)}, f32[16]{0:T(128)}, u32[]{:S(2)}) %copy-start.14) | copy-done | bytes 88
  13.4 0.7 %copy-done.15 = f32[2]{0:T(128)S(1)} copy-done((f32[2]{0:T(128)S(1)}, f32[2]{0:T(128)}, u32[]{:S(2)}) %copy-start.15) | copy-done | bytes 32
  14.0 34.4 %step.1.back = f32[16,8,1024]{2,1,0:T(8,128)S(1)} custom-call(f32[64,2048]{1,0:T(8,128)S(1)} %copy-done.4, f32[5,32768]{1,0:T(8,128)S(1)} %copy-done.2, bf16[8,512,512]{2,1,0:T(8,128)(2,1)} %constant.14.clone.big_hbm, bf16[1024,1280]{1,0:T(8,128)(2,1)S(1)} %copy-done, bf16[6,256,256]{2,1,0:T(8,128)(2,1)S(1)} %copy-done.3, bf16[128,64]{1,0:T(8,128)(2,1)S(1)} %copy-done.9, ...), custom_call_target="tpu_custom_call" | custom-call | tf_op jit(solution)/shard_map/step/pallas_call | solution.py:456
  48.4 0.0 copy-start.1
  48.4 0.8 %copy-done.1 = f32[16,8,1024]{2,1,0:T(8,128)} copy-done((f32[16,8,1024]{2,1,0:T(8,128)}, f32[16,8,1024]{2,1,0:T(8,128)S(1)}, u32[]{:S(2)}) %copy-start.1) | copy-done | bytes 524312
  49.2 1.9 %unpack.1 = f32[64,2048]{1,0:T(8,128)} custom-call(f32[16,8,1024]{2,1,0:T(8,128)} %copy-done.1), custom_call_target="tpu_custom_call" | custom-call | tf_op jit(solution)/shard_map/unpack/pallas_call | solution.py:509
  (11 shorter events, 0.0 us)
Async XLA Ops:
  0.8 1.7 %copy-start = (bf16[1024,1280]{1,0:T(8,128)(2,1)S(1)}, bf16[1024,1280]{1,0:T(8,128)(2,1)}, u32[]{:S(2)}) copy-start(bf16[1024,1280]{1,0:T(8,128)(2,1)} %constant.15.clone.pick_hbm) | copy-start | bytes 7864324
  2.6 1.2 %copy-start.2 = (f32[5,32768]{1,0:T(8,128)S(1)}, f32[5,32768]{1,0:T(8,128)}, u32[]{:S(2)}) copy-start(f32[5,32768]{1,0:T(8,128)} %spectral_hbm.1) | copy-start | bytes 1966084
  3.8 1.1 %copy-start.3 = (bf16[6,256,256]{2,1,0:T(8,128)(2,1)S(1)}, bf16[6,256,256]{2,1,0:T(8,128)(2,1)}, u32[]{:S(2)}) copy-start(bf16[6,256,256]{2,1,0:T(8,128)(2,1)} %constant.16.clone.left) | copy-start | bytes 2359300
  4.9 1.0 %copy-start.4 = (f32[64,2048]{1,0:T(8,128)S(1)}, f32[64,2048]{1,0:T(8,128)}, u32[]{:S(2)}) copy-start(f32[64,2048]{1,0:T(8,128)} %x_hbm.1) | copy-start | bytes 1572868
  6.0 0.9 %copy-start.5 = (f32[32768]{0:T(1024)S(1)}, f32[32768]{0:T(1024)}, u32[]{:S(2)}) copy-start(f32[32768]{0:T(1024)} %param.24) | copy-start | bytes 393220
  6.9 0.9 %copy-start.6 = (bf16[2,32,1024]{2,1,0:T(8,128)(2,1)S(1)}, bf16[2,32,1024]{2,1,0:T(8,128)(2,1)}, u32[]{:S(2)}) copy-start(bf16[2,32,1024]{2,1,0:T(8,128)(2,1)} %constant.20.clone.lanes_in) | copy-start | bytes 393220
  7.8 0.8 %copy-start.7 = (f32[2,32,32]{2,1,0:T(8,128)S(1)}, f32[2,32,32]{2,1,0:T(8,128)}, u32[]{:S(2)}) copy-start(f32[2,32,32]{2,1,0:T(8,128)} %normal.1) | copy-start | bytes 24580
  8.5 0.8 %copy-start.8 = (bf16[128,32]{1,0:T(8,128)(2,1)S(1)}, bf16[128,32]{1,0:T(8,128)(2,1)}, u32[]{:S(2)}) copy-start(bf16[128,32]{1,0:T(8,128)(2,1)} %constant.18.clone.row_out) | copy-start | bytes 24580
  9.3 0.8 %copy-start.9 = (bf16[128,64]{1,0:T(8,128)(2,1)S(1)}, bf16[128,64]{1,0:T(8,128)(2,1)}, u32[]{:S(2)}) copy-start(bf16[128,64]{1,0:T(8,128)(2,1)} %constant.17.clone.spread) | copy-start | bytes 49156
  10.1 0.7 %copy-start.10 = (bf16[32,128]{1,0:T(8,128)(2,1)S(1)}, bf16[32,128]{1,0:T(8,128)(2,1)}, u32[]{:S(2)}) copy-start(bf16[32,128]{1,0:T(8,128)(2,1)} %constant.19.clone.row_in) | copy-start | bytes 24580
  10.8 0.7 %copy-start.11 = (s32[64]{0:T(128)S(1)}, s32[64]{0:T(128)}, u32[]{:S(2)}) copy-start(s32[64]{0:T(128)} %flags.1) | copy-start | bytes 772
  11.4 0.7 %copy-start.12 = (s32[64]{0:T(128)S(1)}, s32[64]{0:T(128)}, u32[]{:S(2)}) copy-start(s32[64]{0:T(128)} %slabs.1) | copy-start | bytes 772
  12.1 0.7 %copy-start.13 = (s32[64]{0:T(128)S(1)}, s32[64]{0:T(128)}, u32[]{:S(2)}) copy-start(s32[64]{0:T(128)} %species.1) | copy-start | bytes 772
  12.7 0.7 %copy-start.14 = (f32[16]{0:T(128)S(1)}, f32[16]{0:T(128)}, u32[]{:S(2)}) copy-start(f32[16]{0:T(128)} %blow.1) | copy-start | bytes 196
  13.4 0.7 %copy-start.15 = (f32[2]{0:T(128)S(1)}, f32[2]{0:T(128)}, u32[]{:S(2)}) copy-start(f32[2]{0:T(128)} %rates.1) | copy-start | bytes 28
  48.4 0.8 %copy-start.1 = (f32[16,8,1024]{2,1,0:T(8,128)}, f32[16,8,1024]{2,1,0:T(8,128)S(1)}, u32[]{:S(2)}) copy-start(f32[16,8,1024]{2,1,0:T(8,128)S(1)} %step.1.back) | copy-start | bytes 1572868
where the time goes:
time: 51.8 us; the launch traced here: 51.1 us
  Pallas kernels  36.2 us (70%)
  local copies, waits for them, and re-layouts  14.8 us (29%)
    pallas_call x1, Pallas kernels, on_device(): pl.pallas_call(kernel, out_shape=jax.ShapeDtypeStruct((VEL, 8, Q), f32),...  34.4 us
    unnamed x33, local copies, waits for them, and re-layouts  14.8 us
    pallas_call x1, Pallas kernels, on_device(): pl.pallas_call(unpack, out_shape=jax.ShapeDtypeStruct((2 * GX, 2 * Q), f3...  1.87 us

commit v1 on v0

v1 whole, which is shorter than its diff:
```python
import functools

import jax
import jax.numpy as jnp
import ml_dtypes
import numpy as np
from jax import lax
from jax.experimental import pallas as pl
from jax.experimental.pallas import tpu as pltpu
from jax.sharding import PartitionSpec as P

NV = 32
GX = 32
Q = NV * NV
HALF = Q // 2
OWN = 4
VEL = 16
SPACE = 8
ROWS = NV * OWN
FACTORS = 5
INPUTS = 17
PLACES = 4
courant = 0.12
top_speed = 4.0
collide_step = 0.5
MESH = pl.DeviceIdType.MESH
f32 = jnp.float32
bf16 = jnp.bfloat16


def parts_of(table):
    hi = table.astype(np.float32).astype(ml_dtypes.bfloat16)
    lo = (table - hi.astype(np.float64)).astype(np.float32).astype(ml_dtypes.bfloat16)
    return hi, lo


def class_slots(parity):
    seen, slots = set(), []
    for kj in range(parity, NV, 2):
        for kl in range(NV):
            other = ((-kj) % NV, (-kl) % NV)
            if other == (kj, kl) or (kj, kl) in seen:
                continue
            seen.add((kj, kl))
            seen.add(other)
            slots.append((kj, kl))
    return slots


def tables():
    j, l = np.divmod(np.arange(HALF), NV)

    def angle(k):
        return 2 * np.pi * ((k[0] * j + k[1] * l) % NV) / NV

    selfs = [((0, 0), (16, 0)), ((0, 16), (16, 16))]
    even, odd = class_slots(0), class_slots(1)
    pair = np.sqrt(2.0) / NV
    t_even = np.zeros((HALF, HALF))
    t_odd = np.zeros((HALF, HALF))
    quarter = HALF // 2
    for n, (a, b) in enumerate(selfs):
        t_even[:, n] = np.cos(angle(a)) / NV
        t_even[:, quarter + n] = np.cos(angle(b)) / NV
    for n, k in enumerate(even):
        t_even[:, n + 2] = pair * np.cos(angle(k))
        t_even[:, quarter + n + 2] = -pair * np.sin(angle(k))
    for n, k in enumerate(odd):
        t_odd[:, n] = pair * np.cos(angle(k))
        t_odd[:, quarter + n] = -pair * np.sin(angle(k))
    big = np.stack(parts_of(t_even) + parts_of(t_odd) + parts_of(t_even.T) + parts_of(t_odd.T))

    phase = 2 * np.pi * (np.outer(np.arange(NV), np.arange(NV)) % NV) / NV
    c = np.kron(np.cos(phase), np.eye(OWN))
    s = np.kron(np.sin(phase), np.eye(OWN))
    fwd = np.block([[c, s], [-s, c]])
    flip = np.block([[c, -s], [-s, -c]])
    inv = np.block([[c, -s], [s, c]])
    left = np.stack([np.concatenate(parts_of(t)) for t in (fwd, flip, inv)])

    w = 0.5 / NV
    width = HALF + 128
    pick = np.zeros((2, Q, width))

    def put(column, k, weight):
        pick[0, k[0] * NV + k[1], column] += weight
        pick[1, ((-k[0]) % NV) * NV + ((-k[1]) % NV), column] += weight

    for n, (a, b) in enumerate(selfs):
        put(n, a, w / 2)
        put(n, b, w / 2)
        put(HALF + n, a, w / 2)
        put(HALF + n, b, -w / 2)
    for n, k in enumerate(even):
        put(n + 2, k, w)
    for n, k in enumerate(odd):
        put(quarter + n, k, w)
    pick = np.concatenate([pick[0], pick[1]], axis=1).astype(ml_dtypes.bfloat16)

    row = np.kron(np.eye(NV), np.ones((OWN, 1)))
    back_row = row[:, (-np.arange(NV)) % NV]
    spread = np.concatenate([row, back_row, row, back_row], axis=1).astype(ml_dtypes.bfloat16)
    row_j = np.kron(np.eye(NV), np.ones((1, NV))).astype(ml_dtypes.bfloat16)
    row_l = np.kron(np.ones((1, NV)), np.eye(NV)).astype(ml_dtypes.bfloat16)
    return big, left, pick, spread, row.astype(ml_dtypes.bfloat16), np.ascontiguousarray(row.T).astype(
        ml_dtypes.bfloat16
    ), np.stack([row_j, row_l])


def split(x):
    hi = x.astype(bf16)
    return hi, (x - hi.astype(f32)).astype(bf16)


def dot(a, b):
    return jnp.dot(a, b, preferred_element_type=f32)


def dot_first(a, b):
    return lax.dot_general(a, b, (((0,), (0,)), ((), ())), preferred_element_type=f32)


def right3(x, table_hi, table_lo):
    hi, lo = x
    both = dot(jnp.concatenate([hi, lo], axis=0), table_hi)
    return both[: hi.shape[0]] + (both[hi.shape[0] :] + dot(hi, table_lo))


def left3(table, x):
    count = table.shape[0] // 2
    both = dot(table, x[0])
    return both[:count] + (both[count:] + dot(table[:count], x[1]))


def kernel(*refs):
    given, (back, *scratch) = refs[:INPUTS], refs[INPUTS:]
    x_hbm = given[0]
    held, scratch = scratch[:INPUTS], scratch[INPUTS:]
    (
        xv,
        spec,
        pick,
        big,
        left,
        spread,
        row_out,
        row_in,
        lanes_in,
        normal,
        tangent,
        emitted,
        flags,
        slabs,
        species,
        blow,
        rates,
    ) = held
    (
        upper,
        lower,
        send,
        recv,
        result,
        spec_rows,
        weights,
        weights_self,
        wall_hi,
        wall_lo,
        part,
        grid_hi,
        grid_lo,
        load_sem,
        keep_sem,
        halo_send,
        halo_recv,
        out_send,
        out_recv,
        back_send,
        back_recv,
    ) = scratch
    space = lax.axis_index("space")
    vel = lax.axis_index("vel")
    place_y, place_x, place_c = vel // 4, (vel // 2) % 2, vel % 2
    after, before = (space + 1) % SPACE, (space + SPACE - 1) % SPACE

    def peer(dy, dx, dc):
        return ((place_y + dy) % 4) * 4 + ((place_x + dx) % 2) * 2 + (place_c + dc) % 2

    offsets = [
        (dy, dx, dc)
        for dy in (2, 1, 3, 0)
        for dx in (1, 0)
        for dc in (1, 0)
        if (dy, dx, dc) != (0, 0, 0)
    ]

    loads = [
        pltpu.make_async_copy(src, dst, load_sem.at[n]) for n, (src, dst) in enumerate(zip(given, held))
    ]
    for load in loads:
        load.start()

    barrier = pltpu.get_barrier_semaphore()
    for step in range(1, VEL):
        pl.semaphore_signal(
            barrier, inc=1, device_id=(space, (vel + step) % VEL), device_id_type=MESH
        )
    for other in (after, before):
        pl.semaphore_signal(barrier, inc=1, device_id=(other, vel), device_id_type=MESH)
    pl.semaphore_wait(barrier, VEL + 1)

    chunks = GX // 8
    first_chunk = (place_y * 2 + place_x) % chunks

    def halo(m, own, number):
        rows = pl.multiple_of(m * 8, 8)
        low = x_hbm.at[pl.ds(rows, 8), pl.ds(own * Q, HALF)]
        high = x_hbm.at[pl.ds(GX + rows, 8), pl.ds(own * Q + HALF, HALF)]
        src, dst, other = ((low, upper, before), (high, lower, after))[number]
        return pltpu.make_async_remote_copy(
            src_ref=src,
            dst_ref=dst.at[own, pl.ds(rows, 8)],
            send_sem=halo_send.at[number, own * chunks + m],
            recv_sem=halo_recv.at[number, own * chunks + m],
            device_id=(other, vel),
            device_id_type=MESH,
        )

    for t in range(chunks):
        for own in range(2):
            for number in range(2):
                halo((first_chunk + t) % chunks, own, number).start()
    loads[0].wait()

    lane = lax.broadcasted_iota(jnp.int32, (1, HALF), 1)
    cell = lax.broadcasted_iota(jnp.int32, (GX, HALF), 0)

    def speed(index):
        return courant * ((2.0 * index.astype(f32) + 1.0 - NV) / NV * top_speed)

    def along_normal(group, half, own):
        at = own * Q + half * HALF
        f = xv[group * GX : (group + 1) * GX, at : at + HALF]
        wall_side = jnp.where(cell == 0, 0.0, pltpu.roll(f, 1, 0))
        far_side = jnp.where(cell == GX - 1, 0.0, pltpu.roll(f, GX - 1, 0))
        a = speed(vel * 2 + own)
        read = f - jnp.maximum(a, 0.0) * (f - wall_side)
        return f, read - jnp.minimum(a, 0.0) * (far_side - f)

    def along_wall(half, f, read, neighbour):
        return read - jnp.abs(speed((lane + half * HALF) // NV)) * (f - neighbour)

    def pack(r0, r1):
        r0, r1 = (r.reshape(r.shape[0] // 8, 8, HALF) for r in (r0, r1))
        sub = lax.broadcasted_iota(jnp.int32, r0.shape, 1)
        first = jnp.where(sub < 4, r0, pltpu.roll(r1, 4, 1))
        return first, jnp.where(sub < 4, pltpu.roll(r0, 4, 1), r1)

    def piece(phase, owner, dest):
        half = (dest // 8 + phase) % 2
        lanes = pl.ds(pl.multiple_of(half * HALF, HALF), HALF)
        return pltpu.make_async_remote_copy(
            src_ref=send.at[dest, :, lanes],
            dst_ref=recv.at[owner, :, lanes],
            send_sem=out_send.at[phase, dest],
            recv_sem=out_recv.at[phase, owner],
            device_id=(space, dest),
            device_id_type=MESH,
        )

    for group in range(2):
        half = group
        at = half * HALF
        other = slice((1 - group) * GX, (2 - group) * GX)
        read = []
        for own in range(2):
            f, along = along_normal(group, half, own)
            neighbour = xv[other, own * Q + at : own * Q + at + HALF]
            read.append(along_wall(half, f, along, neighbour))
        first, second = pack(*read)
        for m in range(chunks):
            send[8 * group + 2 * m, :, at : at + HALF] = first[m]
            send[8 * group + 2 * m + 1, :, at : at + HALF] = second[m]
    for offset in offsets:
        piece(0, vel, peer(*offset)).start()

    for group in range(2):
        for own in range(2):
            part[group, own] = along_normal(group, 1 - group, own)[1]
    for load in loads[1:]:
        load.wait()
    zero3 = jnp.zeros((8 - FACTORS, Q), f32)
    for k in range(NV):
        spec_rows[k] = jnp.concatenate([spec[:, k * Q : (k + 1) * Q], zero3], axis=0)
    width = HALF + 128
    rows_hi, rows_lo = split(
        jnp.concatenate([spec_rows[:, r, :] for r in range(FACTORS)], axis=0)
    )
    both = dot(jnp.concatenate([rows_hi, rows_lo], axis=0), pick[...])
    both = split(both[: FACTORS * NV] + both[FACTORS * NV :])
    for r in range(FACTORS):
        pieces = [b[r * NV : (r + 1) * NV, n * width : (n + 1) * width] for b in both for n in range(2)]
        whole = dot(spread[...], jnp.concatenate(pieces, axis=0))
        weights[r] = whole[:, :HALF]
        weights_self[r] = whole[:, HALF:]

    def second_phase(t, carry):
        m = (first_chunk + t) % chunks
        rows = pl.multiple_of(m * 8, 8)
        for own in range(2):
            for number in range(2):
                halo(m, own, number).wait_recv()
        for group in range(2):
            half = 1 - group
            at = half * HALF
            beside = (lower, upper)[group]
            read = []
            for own in range(2):
                f = xv[pl.ds(group * GX + rows, 8), own * Q + at : own * Q + at + HALF]
                along = part[group, own, pl.ds(rows, 8)]
                read.append(along_wall(half, f, along, beside[own, pl.ds(rows, 8)]))
            first, second = pack(*read)
            send[8 * group + 2 * m, :, at : at + HALF] = first[0]
            send[8 * group + 2 * m + 1, :, at : at + HALF] = second[0]
            for n in range(2):
                dest = 8 * group + 2 * m + n

                @pl.when(dest != vel)
                def _():
                    piece(1, vel, dest).start()

        return carry

    lax.fori_loop(0, chunks, second_phase, 0)
    keep = pltpu.make_async_copy(send.at[vel], recv.at[vel], keep_sem.at[0])
    keep.start()

    row_id = lax.broadcasted_iota(jnp.int32, (ROWS, 1), 0) % OWN
    first_cell = vel * OWN
    rate_column = jnp.zeros((ROWS, 1), f32)
    for c in range(OWN):
        rate = jnp.where(species[first_cell + c] == 1, rates[1], rates[0])
        rate_column = jnp.where(row_id == c, collide_step * rate, rate_column)

    wall_here = vel % 8 == 0
    kind = 0
    slab = 0
    for c in range(OWN):
        kind = kind + flags[first_cell + c] * species[first_cell + c]
        slab = slab + flags[first_cell + c] * slabs[first_cell + c]

    @pl.when(wall_here)
    def _():
        turn = split(jnp.where(kind == 1, tangent[1], tangent[0]))
        by_j = dot_first(turn[0], lanes_in[0]) + dot_first(turn[1], lanes_in[0])
        by_l = dot_first(turn[0], lanes_in[1]) + dot_first(turn[1], lanes_in[1])
        for j in range(NV):
            hi, lo = split(by_j[j : j + 1, :] * by_l)
            wall_hi[j * NV : (j + 1) * NV, :] = hi
            wall_lo[j * NV : (j + 1) * NV, :] = lo

    for phase in range(2):
        for offset in offsets:
            piece(phase, peer(*offset), vel).wait_recv()
    keep.wait()

    @pl.when(wall_here)
    def _():
        scatter = split(jnp.where(kind == 1, normal[1], normal[0]))
        wide = split(dot(row_out[...], scatter[0]) + dot(row_out[...], scatter[1]))
        wide = dot(wide[0], row_in[...]) + dot(wide[1], row_in[...])
        same = row_id == lax.broadcasted_iota(jnp.int32, (1, ROWS), 1) % OWN
        wide = split(jnp.where(same, wide, 0.0))
        x = recv[...].reshape(ROWS, Q)
        turned = split(right3(split(x), wall_hi[...], wall_lo[...]))
        reflected = left3(jnp.concatenate(wide, axis=0), turned)
        gas = jnp.concatenate(
            [emitted[pl.ds(t, NV, stride=Q // 128), :] for t in range(Q // 128)], axis=1
        )
        gas = split(gas)
        gas = dot(row_out[...], gas[0]) + dot(row_out[...], gas[1])
        reflected = reflected + blow[slab] * gas
        flag_column = jnp.zeros((ROWS, 1), jnp.int32)
        for c in range(OWN):
            flag_column = jnp.where(row_id == c, flags[first_cell + c], flag_column)
        recv[...] = jnp.where(flag_column == 1, reflected, x).reshape(VEL, 8, Q)

    quarter = HALF // 2
    xa = recv[:, :, :HALF].reshape(ROWS, HALF)
    xb = recv[:, :, HALF:].reshape(ROWS, HALF)
    ye = right3(split(xa + xb), big[0], big[1])
    yo = right3(split(xa - xb), big[2], big[3])
    z = jnp.concatenate(
        [
            jnp.concatenate([ye[:, :quarter], yo[:, :quarter]], axis=1),
            jnp.concatenate([ye[:, quarter:], yo[:, quarter:]], axis=1),
        ],
        axis=0,
    )
    z = split(z)
    spectrum = left3(left[0], z)
    mirrored = left3(left[1], (z[0][:, :128], z[1][:, :128]))
    for r in range(FACTORS):
        w = jnp.concatenate([weights[r], weights[r]], axis=0)
        d = jnp.concatenate([weights_self[r], weights_self[r]], axis=0)
        scaled = spectrum * w
        first = scaled[:, :128] + mirrored * d
        scaled = split(jnp.concatenate([first, scaled[:, 128:]], axis=1))
        hi, lo = split(left3(left[2], scaled))
        for part, grid in ((hi, grid_hi), (lo, grid_lo)):
            for block in range(2):
                lanes = slice(block * quarter, (block + 1) * quarter)
                grid[block, r, :, :quarter] = part[:ROWS, lanes]
                grid[block, r, :, quarter:] = part[ROWS:, lanes]

    def home(number, dest):
        return pltpu.make_async_remote_copy(
            src_ref=result.at[dest],
            dst_ref=back.at[vel],
            send_sem=back_send.at[number],
            recv_sem=back_recv.at[vel],
            device_id=(space, dest),
            device_id_type=MESH,
        )

    def arrival(owner):
        return pltpu.make_async_remote_copy(
            src_ref=result.at[vel],
            dst_ref=back.at[owner],
            send_sem=back_send.at[0],
            recv_sem=back_recv.at[owner],
            device_id=(space, owner),
            device_id_type=MESH,
        )

    count = ROWS // 4
    rate_part = rate_column[:count]
    for dy in (2, 1, 3, 0):
        plane = (place_y + dy) % 4
        rows = pl.ds(pl.multiple_of(plane * count, count), count)
        sums = []
        for block in range(2):
            lhs = [
                jnp.concatenate([grid[block, r, rows, :] for r in range(FACTORS)], axis=0)
                for grid in (grid_hi, grid_lo)
            ]
            sums.append(right3(lhs, big[4 + 2 * block], big[5 + 2 * block]))
        planes = pl.ds(plane * 4, 4)
        for half, total in ((0, sums[0] + sums[1]), (1, sums[0] - sums[1])):
            filtered = [total[r * count : (r + 1) * count] for r in range(FACTORS)]
            walled = recv[planes, :, half * HALF : (half + 1) * HALF].reshape(count, HALF)
            gained = filtered[0] * filtered[2] + filtered[1] * filtered[3]
            updated = walled + rate_part * (gained - walled * filtered[4])
            result[planes, :, half * HALF : (half + 1) * HALF] = updated.reshape(4, 8, HALF)
        for number, offset in enumerate(offsets):
            if offset[0] == dy:
                home(number, peer(*offset)).start()
    keep = pltpu.make_async_copy(result.at[vel], back.at[vel], keep_sem.at[1])
    keep.start()

    for m in range(chunks):
        for own in range(2):
            for number in range(2):
                halo(m, own, number).wait_send()
    for number, offset in enumerate(offsets):
        for phase in range(2):
            piece(phase, vel, peer(*offset)).wait_send()
        home(number, peer(*offset)).wait_send()
        arrival(peer(*offset)).wait_recv()
    keep.wait()


def place(back, out, held, rows, load_sem, store_sem):
    step = VEL // PLACES
    loads, stores = [], []
    for n in range(PLACES):
        owners = pl.ds(n * step, step)
        cells = pl.ds(n * step * OWN, step * OWN)
        loads.append(pltpu.make_async_copy(back.at[owners], held.at[owners], load_sem.at[n]))
        stores.append(pltpu.make_async_copy(rows.at[cells], out.at[cells], store_sem.at[n]))
        loads[n].start()
    sub = lax.broadcasted_iota(jnp.int32, (8, Q), 0)
    for n in range(PLACES):
        loads[n].wait()
        for m in range(n * step // 2, (n + 1) * step // 2):
            first, second = held[2 * m], held[2 * m + 1]
            rows[8 * m : 8 * m + 8, :Q] = jnp.where(sub < 4, first, pltpu.roll(second, 4, 0))
            rows[8 * m : 8 * m + 8, Q:] = jnp.where(sub < 4, pltpu.roll(first, 4, 0), second)
        stores[n].start()
    for store in stores:
        store.wait()


def on_device(
    distribution,
    wall_flags,
    cell_slab,
    species,
    normal_kernel,
    tangent_kernel,
    blow_rate,
    emitted,
    spectral,
    collide_rate,
):
    big, left, pick, spread, row_out, row_in, lanes_in = (jnp.asarray(t) for t in tables())
    dma = pltpu.SemaphoreType.DMA
    in_vmem = [
        distribution,
        spectral,
        pick,
        big,
        left,
        spread,
        row_out,
        row_in,
        lanes_in,
        normal_kernel,
        tangent_kernel,
        emitted.reshape(NV * Q // 128, 128),
    ]
    in_smem = [wall_flags, cell_slab, species, blow_rate, collide_rate]
    back = pl.pallas_call(
        kernel,
        out_shape=jax.ShapeDtypeStruct((VEL, 8, Q), f32),
        in_specs=[pl.BlockSpec(memory_space=pltpu.HBM)] * INPUTS,
        out_specs=pl.BlockSpec(memory_space=pltpu.HBM),
        scratch_shapes=[pltpu.VMEM(x.shape, x.dtype) for x in in_vmem]
        + [pltpu.SMEM(x.shape, x.dtype) for x in in_smem]
        + [
            pltpu.VMEM((2, GX, HALF), f32),
            pltpu.VMEM((2, GX, HALF), f32),
            pltpu.VMEM((VEL, 8, Q), f32),
            pltpu.VMEM((VEL, 8, Q), f32),
            pltpu.VMEM((VEL, 8, Q), f32),
            pltpu.VMEM((NV, 8, Q), f32),
            pltpu.VMEM((FACTORS, ROWS, HALF), f32),
            pltpu.VMEM((FACTORS, ROWS, 128), f32),
            pltpu.VMEM((Q, Q), bf16),
            pltpu.VMEM((Q, Q), bf16),
            pltpu.VMEM((2, 2, GX, HALF), f32),
            pltpu.VMEM((2, FACTORS, ROWS, HALF), bf16),
            pltpu.VMEM((2, FACTORS, ROWS, HALF), bf16),
            dma((INPUTS,)),
            dma((2,)),
            dma((2, 2 * GX // 8)),
            dma((2, 2 * GX // 8)),
            dma((2, VEL)),
            dma((2, VEL)),
            dma((VEL,)),
            dma((VEL,)),
        ],
        compiler_params=pltpu.CompilerParams(
            collective_id=0, has_side_effects=True, vmem_limit_bytes=56 * 2**20
        ),
        name="step",
    )(*in_vmem, *in_smem)
    return pl.pallas_call(
        place,
        out_shape=jax.ShapeDtypeStruct((2 * GX, 2 * Q), f32),
        in_specs=[pl.BlockSpec(memory_space=pltpu.HBM)],
        out_specs=pl.BlockSpec(memory_space=pltpu.HBM),
        scratch_shapes=[
            pltpu.VMEM((VEL, 8, Q), f32),
            pltpu.VMEM((2 * GX, 2 * Q), f32),
            dma((PLACES,)),
            dma((PLACES,)),
        ],
        compiler_params=pltpu.CompilerParams(vmem_limit_bytes=60 * 2**20),
        name="place",
    )(back)


def solution(mesh):
    in_specs = (P("space", "vel"), P("space"), P("space"), P("space"), P(), P(), P(), P(), P(), P())
    out_specs = P("space", "vel")
    return jax.shard_map(
        on_device, mesh=mesh, in_specs=in_specs, out_specs=out_specs, check_vma=False
    )
```

time: 51.8 us -> 34.2 us (0.66); the launches traced: 51.1 us -> 34 us
  local copies, waits for them, and re-layouts: 14.8 us -> 0 us
  Pallas kernels: 36.2 us -> 34 us
    unnamed x33 -> x0, local copies, waits for them, and re-layouts: 14.8 us -> none
    pallas_call x1, Pallas kernels: 34.4 us -> 32.2 us  [on_device(): pl.pallas_call(kernel, out_shape=jax.ShapeDtypeStruct((VEL, 8, Q), f32),...]
where the time goes in v1:
time: 34.2 us; the launch traced here: 34 us
  Pallas kernels  34 us (99%)
    pallas_call x1, Pallas kernels, on_device(): pl.pallas_call(kernel, out_shape=jax.ShapeDtypeStruct((VEL, 8, Q), f32),...  32.2 us
    pallas_call x1, Pallas kernels, on_device(): pl.pallas_call(place, out_shape=jax.ShapeDtypeStruct((2 * GX, 2 * Q), f32...  1.83 us

profile of v1, /device:TPU:1, one launch (start us, length us, event | category | flops | bytes accessed | tf_op | source)
XLA Modules:
  0.0 34.0 jit_solution(10949664736211879340)
XLA Ops:
  0.0 32.2 %step.1.back = f32[16,8,1024]{2,1,0:T(8,128)} custom-call(f32[64,2048]{1,0:T(8,128)} %refs_0_.1, f32[5,32768]{1,0:T(8,128)} %refs_1_.1, bf16[1024,1280]{1,0:T(8,128)(2,1)} %constant.16.clone.refs_2_, bf16[8,512,512]{2,1,0:T(8,128)(2,1)} %constant.14.clone.refs_3_, bf16[3,512,256]{2,1,0:T(8,128)(2,1)} %constant.15.clone.refs_4_, ...), custom_call_target="tpu_custom_call" | custom-call | tf_op jit(solution)/shard_map/step/pallas_call | solution.py:523
  32.2 1.8 %place.1 = f32[64,2048]{1,0:T(8,128)} custom-call(f32[16,8,1024]{2,1,0:T(8,128)} %step.1.back), custom_call_target="tpu_custom_call" | custom-call | tf_op jit(solution)/shard_map/place/pallas_call | solution.py:558

commit v2 on v1

--- a/solution.py
+++ b/solution.py
@@ -11,15 +11,17 @@
 
 NV = 32
 GX = 32
+WX = 4
 Q = NV * NV
 HALF = Q // 2
-OWN = 4
+BATCHES = 2
+OWN = 2
+BLOCK = 2 * OWN
 VEL = 16
 SPACE = 8
 ROWS = NV * OWN
 FACTORS = 5
 INPUTS = 17
-PLACES = 4
 courant = 0.12
 top_speed = 4.0
 collide_step = 0.5
@@ -76,7 +78,10 @@
     fwd = np.block([[c, s], [-s, c]])
     flip = np.block([[c, -s], [-s, -c]])
     inv = np.block([[c, -s], [s, c]])
-    left = np.stack([np.concatenate(parts_of(t)) for t in (fwd, flip, inv)])
+    left = []
+    for hi, lo in (parts_of(t) for t in (fwd, flip, inv)):
+        left.append(np.block([[hi, hi], [lo, np.zeros_like(lo)]]))
+    left = np.stack(left)
 
     w = 0.5 / NV
     width = HALF + 128
@@ -127,9 +132,9 @@
 
 
 def left3(table, x):
+    both = dot(table, jnp.concatenate(x, axis=0))
     count = table.shape[0] // 2
-    both = dot(table, x[0])
-    return both[:count] + (both[count:] + dot(table[:count], x[1]))
+    return both[:count] + both[count:]
 
 
 def kernel(*refs):
@@ -161,6 +166,8 @@
         send,
         recv,
         result,
+        spectrum,
+        mirrored,
         spec_rows,
         weights,
         weights_self,
@@ -173,6 +180,8 @@
         keep_sem,
         halo_send,
         halo_recv,
+        near_send,
+        near_recv,
         out_send,
         out_recv,
         back_send,
@@ -194,23 +203,22 @@
         if (dy, dx, dc) != (0, 0, 0)
     ]
 
+    barrier = pltpu.get_barrier_semaphore()
+    for other in (after, before):
+        pl.semaphore_signal(barrier, inc=1, device_id=(other, vel), device_id_type=MESH)
+    for offset in offsets:
+        pl.semaphore_signal(barrier, inc=1, device_id=(space, peer(*offset)), device_id_type=MESH)
+
     loads = [
         pltpu.make_async_copy(src, dst, load_sem.at[n]) for n, (src, dst) in enumerate(zip(given, held))
     ]
-    for load in loads:
-        load.start()
-
-    barrier = pltpu.get_barrier_semaphore()
-    for step in range(1, VEL):
-        pl.semaphore_signal(
-            barrier, inc=1, device_id=(space, (vel + step) % VEL), device_id_type=MESH
-        )
-    for other in (after, before):
-        pl.semaphore_signal(barrier, inc=1, device_id=(other, vel), device_id_type=MESH)
+    loads[0].start()
     pl.semaphore_wait(barrier, VEL + 1)
 
     chunks = GX // 8
-    first_chunk = (place_y * 2 + place_x) % chunks
+
+    def chunk(step):
+        return 2 * (step // 2) + (step + place_y) % 2
 
     def halo(m, own, number):
         rows = pl.multiple_of(m * 8, 8)
@@ -229,7 +237,9 @@
     for t in range(chunks):
         for own in range(2):
             for number in range(2):
-                halo((first_chunk + t) % chunks, own, number).start()
+                halo(chunk(t), own, number).start()
+    for load in loads[1:]:
+        load.start()
     loads[0].wait()
 
     lane = lax.broadcasted_iota(jnp.int32, (1, HALF), 1)
@@ -250,20 +260,33 @@
     def along_wall(half, f, read, neighbour):
         return read - jnp.abs(speed((lane + half * HALF) // NV)) * (f - neighbour)
 
-    def pack(r0, r1):
-        r0, r1 = (r.reshape(r.shape[0] // 8, 8, HALF) for r in (r0, r1))
-        sub = lax.broadcasted_iota(jnp.int32, r0.shape, 1)
-        first = jnp.where(sub < 4, r0, pltpu.roll(r1, 4, 1))
-        return first, jnp.where(sub < 4, pltpu.roll(r0, 4, 1), r1)
-
-    def piece(phase, owner, dest):
-        half = (dest // 8 + phase) % 2
-        lanes = pl.ds(pl.multiple_of(half * HALF, HALF), HALF)
+    def pack(group, m, lanes, r0, r1):
+        for k in range(4):
+            pair = slice(OWN * k, OWN * k + OWN)
+            block = jnp.concatenate([r0[pair], r1[pair]], axis=0)
+            send[m // 2, 8 * group + 4 * (m % 2) + k, :, lanes] = block
+
+    def lanes_of(half):
+        return pl.ds(pl.multiple_of(half * HALF, HALF), HALF)
+
+    def near(owner, dest):
+        lanes = lanes_of(dest // 8)
         return pltpu.make_async_remote_copy(
-            src_ref=send.at[dest, :, lanes],
-            dst_ref=recv.at[owner, :, lanes],
-            send_sem=out_send.at[phase, dest],
-            recv_sem=out_recv.at[phase, owner],
+            src_ref=send.at[:, dest, :, lanes],
+            dst_ref=recv.at[:, owner, :, lanes],
+            send_sem=near_send.at[dest],
+            recv_sem=near_recv.at[owner],
+            device_id=(space, dest),
+            device_id_type=MESH,
+        )
+
+    def far(batch, owner, dest):
+        lanes = lanes_of(1 - dest // 8)
+        return pltpu.make_async_remote_copy(
+            src_ref=send.at[batch, dest, :, lanes],
+            dst_ref=recv.at[batch, owner, :, lanes],
+            send_sem=out_send.at[batch, dest],
+            recv_sem=out_recv.at[batch, owner],
             device_id=(space, dest),
             device_id_type=MESH,
         )
@@ -277,12 +300,10 @@
             f, along = along_normal(group, half, own)
             neighbour = xv[other, own * Q + at : own * Q + at + HALF]
             read.append(along_wall(half, f, along, neighbour))
-        first, second = pack(*read)
         for m in range(chunks):
-            send[8 * group + 2 * m, :, at : at + HALF] = first[m]
-            send[8 * group + 2 * m + 1, :, at : at + HALF] = second[m]
+            pack(group, m, slice(at, at + HALF), *(r[8 * m : 8 * m + 8] for r in read))
     for offset in offsets:
-        piece(0, vel, peer(*offset)).start()
+        near(vel, peer(*offset)).start()
 
     for group in range(2):
         for own in range(2):
@@ -305,7 +326,7 @@
         weights_self[r] = whole[:, HALF:]
 
     def second_phase(t, carry):
-        m = (first_chunk + t) % chunks
+        m = chunk(t)
         rows = pl.multiple_of(m * 8, 8)
         for own in range(2):
             for number in range(2):
@@ -319,30 +340,23 @@
                 f = xv[pl.ds(group * GX + rows, 8), own * Q + at : own * Q + at + HALF]
                 along = part[group, own, pl.ds(rows, 8)]
                 read.append(along_wall(half, f, along, beside[own, pl.ds(rows, 8)]))
-            first, second = pack(*read)
-            send[8 * group + 2 * m, :, at : at + HALF] = first[0]
-            send[8 * group + 2 * m + 1, :, at : at + HALF] = second[0]
-            for n in range(2):
-                dest = 8 * group + 2 * m + n
+            pack(group, m, slice(at, at + HALF), *read)
+            for k in range(4):
+                dest = 8 * group + 4 * (m % 2) + k
 
                 @pl.when(dest != vel)
                 def _():
-                    piece(1, vel, dest).start()
+                    far(m // 2, vel, dest).start()
 
         return carry
 
     lax.fori_loop(0, chunks, second_phase, 0)
-    keep = pltpu.make_async_copy(send.at[vel], recv.at[vel], keep_sem.at[0])
+    keep = pltpu.make_async_copy(send.at[:, vel], recv.at[:, vel], keep_sem.at[0])
     keep.start()
 
     row_id = lax.broadcasted_iota(jnp.int32, (ROWS, 1), 0) % OWN
-    first_cell = vel * OWN
-    rate_column = jnp.zeros((ROWS, 1), f32)
-    for c in range(OWN):
-        rate = jnp.where(species[first_cell + c] == 1, rates[1], rates[0])
-        rate_column = jnp.where(row_id == c, collide_step * rate, rate_column)
-
-    wall_here = vel % 8 == 0
+    first_cell = (vel // 8) * GX + (vel % 8) * OWN
+    wall_here = vel % 8 < WX // OWN
     kind = 0
     slab = 0
     for c in range(OWN):
@@ -359,133 +373,161 @@
             wall_hi[j * NV : (j + 1) * NV, :] = hi
             wall_lo[j * NV : (j + 1) * NV, :] = lo
 
-    for phase in range(2):
-        for offset in offsets:
-            piece(phase, peer(*offset), vel).wait_recv()
-    keep.wait()
-
-    @pl.when(wall_here)
-    def _():
-        scatter = split(jnp.where(kind == 1, normal[1], normal[0]))
-        wide = split(dot(row_out[...], scatter[0]) + dot(row_out[...], scatter[1]))
-        wide = dot(wide[0], row_in[...]) + dot(wide[1], row_in[...])
-        same = row_id == lax.broadcasted_iota(jnp.int32, (1, ROWS), 1) % OWN
-        wide = split(jnp.where(same, wide, 0.0))
-        x = recv[...].reshape(ROWS, Q)
-        turned = split(right3(split(x), wall_hi[...], wall_lo[...]))
-        reflected = left3(jnp.concatenate(wide, axis=0), turned)
-        gas = jnp.concatenate(
-            [emitted[pl.ds(t, NV, stride=Q // 128), :] for t in range(Q // 128)], axis=1
-        )
-        gas = split(gas)
-        gas = dot(row_out[...], gas[0]) + dot(row_out[...], gas[1])
-        reflected = reflected + blow[slab] * gas
-        flag_column = jnp.zeros((ROWS, 1), jnp.int32)
-        for c in range(OWN):
-            flag_column = jnp.where(row_id == c, flags[first_cell + c], flag_column)
-        recv[...] = jnp.where(flag_column == 1, reflected, x).reshape(VEL, 8, Q)
-
-    quarter = HALF // 2
-    xa = recv[:, :, :HALF].reshape(ROWS, HALF)
-    xb = recv[:, :, HALF:].reshape(ROWS, HALF)
-    ye = right3(split(xa + xb), big[0], big[1])
-    yo = right3(split(xa - xb), big[2], big[3])
-    z = jnp.concatenate(
-        [
-            jnp.concatenate([ye[:, :quarter], yo[:, :quarter]], axis=1),
-            jnp.concatenate([ye[:, quarter:], yo[:, quarter:]], axis=1),
-        ],
-        axis=0,
-    )
-    z = split(z)
-    spectrum = left3(left[0], z)
-    mirrored = left3(left[1], (z[0][:, :128], z[1][:, :128]))
-    for r in range(FACTORS):
-        w = jnp.concatenate([weights[r], weights[r]], axis=0)
-        d = jnp.concatenate([weights_self[r], weights_self[r]], axis=0)
-        scaled = spectrum * w
-        first = scaled[:, :128] + mirrored * d
-        scaled = split(jnp.concatenate([first, scaled[:, 128:]], axis=1))
-        hi, lo = split(left3(left[2], scaled))
-        for part, grid in ((hi, grid_hi), (lo, grid_lo)):
-            for block in range(2):
-                lanes = slice(block * quarter, (block + 1) * quarter)
-                grid[block, r, :, :quarter] = part[:ROWS, lanes]
-                grid[block, r, :, quarter:] = part[ROWS:, lanes]
-
-    def home(number, dest):
+    def home(batch, dest):
         return pltpu.make_async_remote_copy(
-            src_ref=result.at[dest],
-            dst_ref=back.at[vel],
-            send_sem=back_send.at[number],
-            recv_sem=back_recv.at[vel],
+            src_ref=result.at[batch, dest],
+            dst_ref=back.at[batch, vel],
+            send_sem=back_send.at[batch, dest],
+            recv_sem=back_recv.at[batch, vel],
             device_id=(space, dest),
             device_id_type=MESH,
         )
 
-    def arrival(owner):
+    def arrival(batch, owner):
         return pltpu.make_async_remote_copy(
-            src_ref=result.at[vel],
-            dst_ref=back.at[owner],
-            send_sem=back_send.at[0],
-            recv_sem=back_recv.at[owner],
+            src_ref=result.at[batch, vel],
+            dst_ref=back.at[batch, owner],
+            send_sem=back_send.at[batch, owner],
+            recv_sem=back_recv.at[batch, owner],
             device_id=(space, owner),
             device_id_type=MESH,
         )
 
-    count = ROWS // 4
-    rate_part = rate_column[:count]
-    for dy in (2, 1, 3, 0):
-        plane = (place_y + dy) % 4
-        rows = pl.ds(pl.multiple_of(plane * count, count), count)
-        sums = []
-        for block in range(2):
-            lhs = [
-                jnp.concatenate([grid[block, r, rows, :] for r in range(FACTORS)], axis=0)
-                for grid in (grid_hi, grid_lo)
-            ]
-            sums.append(right3(lhs, big[4 + 2 * block], big[5 + 2 * block]))
-        planes = pl.ds(plane * 4, 4)
-        for half, total in ((0, sums[0] + sums[1]), (1, sums[0] - sums[1])):
-            filtered = [total[r * count : (r + 1) * count] for r in range(FACTORS)]
-            walled = recv[planes, :, half * HALF : (half + 1) * HALF].reshape(count, HALF)
-            gained = filtered[0] * filtered[2] + filtered[1] * filtered[3]
-            updated = walled + rate_part * (gained - walled * filtered[4])
-            result[planes, :, half * HALF : (half + 1) * HALF] = updated.reshape(4, 8, HALF)
-        for number, offset in enumerate(offsets):
-            if offset[0] == dy:
-                home(number, peer(*offset)).start()
-    keep = pltpu.make_async_copy(result.at[vel], back.at[vel], keep_sem.at[1])
+    for offset in offsets:
+        near(peer(*offset), vel).wait_recv()
+    keep.wait()
+    quarter = HALF // 2
+    count = ROWS // 2
+
+    def collide(batch, carry):
+        for offset in offsets:
+            far(batch, peer(*offset), vel).wait_recv()
+
+        @pl.when(jnp.logical_and(wall_here, batch == 0))
+        def _():
+            scatter = split(jnp.where(kind == 1, normal[1], normal[0]))
+            wide = split(dot(row_out[...], scatter[0]) + dot(row_out[...], scatter[1]))
+            wide = dot(wide[0], row_in[...]) + dot(wide[1], row_in[...])
+            same = row_id == lax.broadcasted_iota(jnp.int32, (1, ROWS), 1) % OWN
+            wide = split(jnp.where(same, wide, 0.0))
+            x = recv[0].reshape(ROWS, Q)
+            turned = split(right3(split(x), wall_hi[...], wall_lo[...]))
+            reflected = dot(wide[0], turned[0]) + (dot(wide[1], turned[0]) + dot(wide[0], turned[1]))
+            gas = jnp.concatenate(
+                [emitted[pl.ds(t, NV, stride=Q // 128), :] for t in range(Q // 128)], axis=1
+            )
+            gas = split(gas)
+            gas = dot(row_out[...], gas[0]) + dot(row_out[...], gas[1])
+            reflected = reflected + blow[slab] * gas
+            flag_column = jnp.zeros((ROWS, 1), jnp.int32)
+            for c in range(OWN):
+                flag_column = jnp.where(row_id == c, flags[first_cell + c], flag_column)
+            recv[0] = jnp.where(flag_column == 1, reflected, x).reshape(VEL, BLOCK, Q)
+
+        rate_part = jnp.zeros((count, 1), f32)
+        for c in range(OWN):
+            kind_here = species[first_cell + batch * (GX // BATCHES) + c]
+            rate = jnp.where(kind_here == 1, rates[1], rates[0])
+            rate_part = jnp.where(row_id[:count] == c, collide_step * rate, rate_part)
+
+        xa = recv[batch, :, :, :HALF].reshape(ROWS, HALF)
+        xb = recv[batch, :, :, HALF:].reshape(ROWS, HALF)
+        ye = right3(split(xa + xb), big[0], big[1])
+        yo = right3(split(xa - xb), big[2], big[3])
+        z = jnp.concatenate(
+            [
+                jnp.concatenate([ye[:, :quarter], yo[:, :quarter]], axis=1),
+                jnp.concatenate([ye[:, quarter:], yo[:, quarter:]], axis=1),
+            ],
+            axis=0,
+        )
+        z = split(z)
+        spectrum[...] = left3(left[0], z)
+        mirrored[...] = left3(left[1], (z[0][:, :128], z[1][:, :128]))
+
+        def weigh(r, carry):
+            w = jnp.concatenate([weights[r], weights[r]], axis=0)
+            d = jnp.concatenate([weights_self[r], weights_self[r]], axis=0)
+            scaled = spectrum[...] * w
+            first = scaled[:, :128] + mirrored[...] * d
+            scaled = split(jnp.concatenate([first, scaled[:, 128:]], axis=1))
+            hi, lo = split(left3(left[2], scaled))
+            for part_, grid in ((hi, grid_hi), (lo, grid_lo)):
+                for block in range(2):
+                    lanes = slice(block * quarter, (block + 1) * quarter)
+                    grid[block, r, :, :quarter] = part_[:ROWS, lanes]
+                    grid[block, r, :, quarter:] = part_[ROWS:, lanes]
+            return carry
+
+        for r in range(FACTORS):
+            weigh(r, 0)
+
+        def restore(step, carry):
+            side = (place_y // 2 + 1 + step) % 2
+            rows = pl.ds(pl.multiple_of(side * count, count), count)
+            sums = []
+            for block in range(2):
+                lhs = [
+                    jnp.concatenate([grid[block, r, rows, :] for r in range(FACTORS)], axis=0)
+                    for grid in (grid_hi, grid_lo)
+                ]
+                sums.append(right3(lhs, big[4 + 2 * block], big[5 + 2 * block]))
+            owners = pl.ds(side * (VEL // 2), VEL // 2)
+            for half, total in ((0, sums[0] + sums[1]), (1, sums[0] - sums[1])):
+                filtered = [total[r * count : (r + 1) * count] for r in range(FACTORS)]
+                lanes = slice(half * HALF, (half + 1) * HALF)
+                walled = recv[batch, owners, :, lanes].reshape(count, HALF)
+                gained = filtered[0] * filtered[2] + filtered[1] * filtered[3]
+                updated = walled + rate_part * (gained - walled * filtered[4])
+                result[batch, owners, :, lanes] = updated.reshape(VEL // 2, BLOCK, HALF)
+            for plane in range(2):
+                for dx in (1, 0):
+                    for dc in (1, 0):
+                        dest = (side * 2 + (place_y + plane) % 2) * 4
+                        dest = dest + ((place_x + dx) % 2) * 2 + (place_c + dc) % 2
+
+                        @pl.when(dest != vel)
+                        def _():
+                            home(batch, dest).start()
+
+            return carry
+
+        for step in range(2):
+            restore(step, 0)
+        return carry
+
+    for batch in range(BATCHES):
+        collide(batch, 0)
+    keep = pltpu.make_async_copy(result.at[:, vel], back.at[:, vel], keep_sem.at[1])
     keep.start()
 
     for m in range(chunks):
         for own in range(2):
             for number in range(2):
                 halo(m, own, number).wait_send()
-    for number, offset in enumerate(offsets):
-        for phase in range(2):
-            piece(phase, vel, peer(*offset)).wait_send()
-        home(number, peer(*offset)).wait_send()
-        arrival(peer(*offset)).wait_recv()
+    for offset in offsets:
+        near(vel, peer(*offset)).wait_send()
+        for batch in range(BATCHES):
+            far(batch, vel, peer(*offset)).wait_send()
+            home(batch, peer(*offset)).wait_send()
+            arrival(batch, peer(*offset)).wait_recv()
     keep.wait()
 
 
 def place(back, out, held, rows, load_sem, store_sem):
-    step = VEL // PLACES
     loads, stores = [], []
-    for n in range(PLACES):
-        owners = pl.ds(n * step, step)
-        cells = pl.ds(n * step * OWN, step * OWN)
-        loads.append(pltpu.make_async_copy(back.at[owners], held.at[owners], load_sem.at[n]))
+    for n in range(GX // 4):
+        group, m = n // 4, n % 4
+        owners = (m // 2, pl.ds(8 * group + 4 * (m % 2), 4))
+        cells = pl.ds(8 * n, 8)
+        loads.append(pltpu.make_async_copy(back.at[owners], held.at[n], load_sem.at[n]))
         stores.append(pltpu.make_async_copy(rows.at[cells], out.at[cells], store_sem.at[n]))
         loads[n].start()
-    sub = lax.broadcasted_iota(jnp.int32, (8, Q), 0)
-    for n in range(PLACES):
+    for n in range(GX // 4):
         loads[n].wait()
-        for m in range(n * step // 2, (n + 1) * step // 2):
-            first, second = held[2 * m], held[2 * m + 1]
-            rows[8 * m : 8 * m + 8, :Q] = jnp.where(sub < 4, first, pltpu.roll(second, 4, 0))
-            rows[8 * m : 8 * m + 8, Q:] = jnp.where(sub < 4, pltpu.roll(first, 4, 0), second)
+        for own in range(2):
+            block = [held[n, k, own * OWN : (own + 1) * OWN, :] for k in range(4)]
+            rows[8 * n : 8 * n + 8, own * Q : (own + 1) * Q] = jnp.concatenate(block, axis=0)
         stores[n].start()
     for store in stores:
         store.wait()
@@ -522,7 +564,7 @@
     in_smem = [wall_flags, cell_slab, species, blow_rate, collide_rate]
     back = pl.pallas_call(
         kernel,
-        out_shape=jax.ShapeDtypeStruct((VEL, 8, Q), f32),
+        out_shape=jax.ShapeDtypeStruct((BATCHES, VEL, BLOCK, Q), f32),
         in_specs=[pl.BlockSpec(memory_space=pltpu.HBM)] * INPUTS,
         out_specs=pl.BlockSpec(memory_space=pltpu.HBM),
         scratch_shapes=[pltpu.VMEM(x.shape, x.dtype) for x in in_vmem]
@@ -530,9 +572,11 @@
         + [
             pltpu.VMEM((2, GX, HALF), f32),
             pltpu.VMEM((2, GX, HALF), f32),
-            pltpu.VMEM((VEL, 8, Q), f32),
-            pltpu.VMEM((VEL, 8, Q), f32),
-            pltpu.VMEM((VEL, 8, Q), f32),
+            pltpu.VMEM((BATCHES, VEL, BLOCK, Q), f32),
+            pltpu.VMEM((BATCHES, VEL, BLOCK, Q), f32),
+            pltpu.VMEM((BATCHES, VEL, BLOCK, Q), f32),
+            pltpu.VMEM((2 * ROWS, HALF), f32),
+            pltpu.VMEM((2 * ROWS, 128), f32),
             pltpu.VMEM((NV, 8, Q), f32),
             pltpu.VMEM((FACTORS, ROWS, HALF), f32),
             pltpu.VMEM((FACTORS, ROWS, 128), f32),
@@ -545,10 +589,12 @@
             dma((2,)),
             dma((2, 2 * GX // 8)),
             dma((2, 2 * GX // 8)),
-            dma((2, VEL)),
-            dma((2, VEL)),
             dma((VEL,)),
             dma((VEL,)),
+            dma((BATCHES, VEL)),
+            dma((BATCHES, VEL)),
+            dma((BATCHES, VEL)),
+            dma((BATCHES, VEL)),
         ],
         compiler_params=pltpu.CompilerParams(
             collective_id=0, has_side_effects=True, vmem_limit_bytes=56 * 2**20
@@ -561,10 +607,10 @@
         in_specs=[pl.BlockSpec(memory_space=pltpu.HBM)],
         out_specs=pl.BlockSpec(memory_space=pltpu.HBM),
         scratch_shapes=[
-            pltpu.VMEM((VEL, 8, Q), f32),
+            pltpu.VMEM((GX // 4, 4, BLOCK, Q), f32),
             pltpu.VMEM((2 * GX, 2 * Q), f32),
-            dma((PLACES,)),
-            dma((PLACES,)),
+            dma((GX // 4,)),
+            dma((GX // 4,)),
         ],
         compiler_params=pltpu.CompilerParams(vmem_limit_bytes=60 * 2**20),
         name="place",

time: 34.2 us -> 32.5 us (0.950)
  Pallas kernels: 34 us -> 32.4 us
    pallas_call x1, Pallas kernels: 32.2 us -> 30.5 us  [on_device(): pl.pallas_call(kernel, out_shape=jax.ShapeDtypeStruct((BATCHES, VEL, BLOC...]
where the time goes in v2:
time: 32.5 us; the launch traced here: 32.4 us
  Pallas kernels  32.4 us (100%)
    pallas_call x1, Pallas kernels, on_device(): pl.pallas_call(kernel, out_shape=jax.ShapeDtypeStruct((BATCHES, VEL, BLOC...  30.5 us
    pallas_call x1, Pallas kernels, on_device(): pl.pallas_call(place, out_shape=jax.ShapeDtypeStruct((2 * GX, 2 * Q), f32...  1.85 us

profile of v2, /device:TPU:1, one launch (start us, length us, event | category | flops | bytes accessed | tf_op | source)
XLA Modules:
  0.0 32.4 jit_solution(14729737247669490726)
XLA Ops:
  0.0 30.5 %step.1.back = f32[2,16,4,1024]{3,2,1,0:T(4,128)} custom-call(f32[64,2048]{1,0:T(8,128)} %refs_0_.1, f32[5,32768]{1,0:T(8,128)} %refs_1_.1, bf16[1024,1280]{1,0:T(8,128)(2,1)} %constant.16.clone.refs_2_, bf16[8,512,512]{2,1,0:T(8,128)(2,1)} %constant.14.clone.refs_3_, bf16[3,256,256]{2,1,0:T(8,128)(2,1)} %constant.15.clone.refs_4_, ...), custom_call_target="tpu_custom_call" | custom-call | tf_op jit(solution)/shard_map/step/pallas_call | solution.py:565
  30.5 1.8 %place.1 = f32[64,2048]{1,0:T(8,128)} custom-call(f32[2,16,4,1024]{3,2,1,0:T(4,128)} %step.1.back), custom_call_target="tpu_custom_call" | custom-call | tf_op jit(solution)/shard_map/place/pallas_call | solution.py:604

commit v3 on v2

--- a/solution.py
+++ b/solution.py
@@ -21,7 +21,7 @@
 SPACE = 8
 ROWS = NV * OWN
 FACTORS = 5
-INPUTS = 17
+INPUTS = 18
 courant = 0.12
 top_speed = 4.0
 collide_step = 0.5
@@ -36,9 +36,9 @@
     return hi, lo
 
 
-def class_slots(parity):
+def class_slots(first, step):
     seen, slots = set(), []
-    for kj in range(parity, NV, 2):
+    for kj in range(first, NV, step):
         for kl in range(NV):
             other = ((-kj) % NV, (-kl) % NV)
             if other == (kj, kl) or (kj, kl) in seen:
@@ -56,21 +56,30 @@
         return 2 * np.pi * ((k[0] * j + k[1] * l) % NV) / NV
 
     selfs = [((0, 0), (16, 0)), ((0, 16), (16, 16))]
-    even, odd = class_slots(0), class_slots(1)
+    zero, two, odd = class_slots(0, 4), class_slots(2, 4), class_slots(1, 2)
     pair = np.sqrt(2.0) / NV
-    t_even = np.zeros((HALF, HALF))
+    quarter = HALF // 2
+    eighth = quarter // 2
+    t_zero = np.zeros((HALF, quarter))
+    t_two = np.zeros((HALF, quarter))
     t_odd = np.zeros((HALF, HALF))
-    quarter = HALF // 2
     for n, (a, b) in enumerate(selfs):
-        t_even[:, n] = np.cos(angle(a)) / NV
-        t_even[:, quarter + n] = np.cos(angle(b)) / NV
-    for n, k in enumerate(even):
-        t_even[:, n + 2] = pair * np.cos(angle(k))
-        t_even[:, quarter + n + 2] = -pair * np.sin(angle(k))
+        t_zero[:, n] = np.cos(angle(a)) / NV
+        t_zero[:, eighth + n] = np.cos(angle(b)) / NV
+    for n, k in enumerate(zero):
+        t_zero[:, n + 2] = pair * np.cos(angle(k))
+        t_zero[:, eighth + n + 2] = -pair * np.sin(angle(k))
+    for n, k in enumerate(two):
+        t_two[:, n] = pair * np.cos(angle(k))
+        t_two[:, eighth + n] = -pair * np.sin(angle(k))
     for n, k in enumerate(odd):
         t_odd[:, n] = pair * np.cos(angle(k))
         t_odd[:, quarter + n] = -pair * np.sin(angle(k))
-    big = np.stack(parts_of(t_even) + parts_of(t_odd) + parts_of(t_even.T) + parts_of(t_odd.T))
+    t_zero, t_two = t_zero[:quarter], t_two[:quarter]
+    big = np.stack(parts_of(t_odd) + parts_of(t_odd.T))
+    small = np.stack(
+        parts_of(t_zero) + parts_of(t_two) + parts_of(t_zero.T) + parts_of(t_two.T)
+    )
 
     phase = 2 * np.pi * (np.outer(np.arange(NV), np.arange(NV)) % NV) / NV
     c = np.kron(np.cos(phase), np.eye(OWN))
@@ -96,8 +105,10 @@
         put(n, b, w / 2)
         put(HALF + n, a, w / 2)
         put(HALF + n, b, -w / 2)
-    for n, k in enumerate(even):
+    for n, k in enumerate(zero):
         put(n + 2, k, w)
+    for n, k in enumerate(two):
+        put(eighth + n, k, w)
     for n, k in enumerate(odd):
         put(quarter + n, k, w)
     pick = np.concatenate([pick[0], pick[1]], axis=1).astype(ml_dtypes.bfloat16)
@@ -107,7 +118,7 @@
     spread = np.concatenate([row, back_row, row, back_row], axis=1).astype(ml_dtypes.bfloat16)
     row_j = np.kron(np.eye(NV), np.ones((1, NV))).astype(ml_dtypes.bfloat16)
     row_l = np.kron(np.ones((1, NV)), np.eye(NV)).astype(ml_dtypes.bfloat16)
-    return big, left, pick, spread, row.astype(ml_dtypes.bfloat16), np.ascontiguousarray(row.T).astype(
+    return big, small, left, pick, spread, row.astype(ml_dtypes.bfloat16), np.ascontiguousarray(row.T).astype(
         ml_dtypes.bfloat16
     ), np.stack([row_j, row_l])
 
@@ -146,6 +157,7 @@
         spec,
         pick,
         big,
+        small,
         left,
         spread,
         row_out,
@@ -341,7 +353,8 @@
                 along = part[group, own, pl.ds(rows, 8)]
                 read.append(along_wall(half, f, along, beside[own, pl.ds(rows, 8)]))
             pack(group, m, slice(at, at + HALF), *read)
-            for k in range(4):
+            for dx, dc in ((1, 1), (1, 0), (0, 1), (0, 0)):
+                k = ((place_x + dx) % 2) * 2 + (place_c + dc) % 2
                 dest = 8 * group + 4 * (m % 2) + k
 
                 @pl.when(dest != vel)
@@ -397,6 +410,7 @@
         near(peer(*offset), vel).wait_recv()
     keep.wait()
     quarter = HALF // 2
+    eighth = quarter // 2
     count = ROWS // 2
 
     def collide(batch, carry):
@@ -432,12 +446,15 @@
 
         xa = recv[batch, :, :, :HALF].reshape(ROWS, HALF)
         xb = recv[batch, :, :, HALF:].reshape(ROWS, HALF)
-        ye = right3(split(xa + xb), big[0], big[1])
-        yo = right3(split(xa - xb), big[2], big[3])
+        even = xa + xb
+        low, high = even[:, :quarter], even[:, quarter:]
+        y0 = right3(split(low + high), small[0], small[1])
+        y2 = right3(split(low - high), small[2], small[3])
+        yo = right3(split(xa - xb), big[0], big[1])
         z = jnp.concatenate(
             [
-                jnp.concatenate([ye[:, :quarter], yo[:, :quarter]], axis=1),
-                jnp.concatenate([ye[:, quarter:], yo[:, quarter:]], axis=1),
+                jnp.concatenate([y0[:, :eighth], y2[:, :eighth], yo[:, :quarter]], axis=1),
+                jnp.concatenate([y0[:, eighth:], y2[:, eighth:], yo[:, quarter:]], axis=1),
             ],
             axis=0,
         )
@@ -453,10 +470,12 @@
             scaled = split(jnp.concatenate([first, scaled[:, 128:]], axis=1))
             hi, lo = split(left3(left[2], scaled))
             for part_, grid in ((hi, grid_hi), (lo, grid_lo)):
-                for block in range(2):
-                    lanes = slice(block * quarter, (block + 1) * quarter)
-                    grid[block, r, :, :quarter] = part_[:ROWS, lanes]
-                    grid[block, r, :, quarter:] = part_[ROWS:, lanes]
+                for n in range(2):
+                    lanes = slice(n * eighth, (n + 1) * eighth)
+                    grid[0, r, :, n * quarter : n * quarter + eighth] = part_[:ROWS, lanes]
+                    grid[0, r, :, n * quarter + eighth : (n + 1) * quarter] = part_[ROWS:, lanes]
+                grid[1, r, :, :quarter] = part_[:ROWS, quarter:]
+                grid[1, r, :, quarter:] = part_[ROWS:, quarter:]
             return carry
 
         for r in range(FACTORS):
@@ -465,15 +484,18 @@
         def restore(step, carry):
             side = (place_y // 2 + 1 + step) % 2
             rows = pl.ds(pl.multiple_of(side * count, count), count)
-            sums = []
-            for block in range(2):
-                lhs = [
-                    jnp.concatenate([grid[block, r, rows, :] for r in range(FACTORS)], axis=0)
+            def rows_of(block, lanes):
+                return [
+                    jnp.concatenate([grid[block, r, rows, lanes] for r in range(FACTORS)], axis=0)
                     for grid in (grid_hi, grid_lo)
                 ]
-                sums.append(right3(lhs, big[4 + 2 * block], big[5 + 2 * block]))
+
+            e0 = right3(rows_of(0, slice(0, quarter)), small[4], small[5])
+            e2 = right3(rows_of(0, slice(quarter, HALF)), small[6], small[7])
+            even = jnp.concatenate([e0 + e2, e0 - e2], axis=1)
+            odd = right3(rows_of(1, slice(0, HALF)), big[2], big[3])
             owners = pl.ds(side * (VEL // 2), VEL // 2)
-            for half, total in ((0, sums[0] + sums[1]), (1, sums[0] - sums[1])):
+            for half, total in ((0, even + odd), (1, even - odd)):
                 filtered = [total[r * count : (r + 1) * count] for r in range(FACTORS)]
                 lanes = slice(half * HALF, (half + 1) * HALF)
                 walled = recv[batch, owners, :, lanes].reshape(count, HALF)
@@ -545,13 +567,14 @@
     spectral,
     collide_rate,
 ):
-    big, left, pick, spread, row_out, row_in, lanes_in = (jnp.asarray(t) for t in tables())
+    big, small, left, pick, spread, row_out, row_in, lanes_in = (jnp.asarray(t) for t in tables())
     dma = pltpu.SemaphoreType.DMA
     in_vmem = [
         distribution,
         spectral,
         pick,
         big,
+        small,
         left,
         spread,
         row_out,

time: 32.5 us -> 32.5 us (level)
  no operation moved by 1% of the time
where the time goes in v3:
time: 32.5 us; the launch traced here: 32.4 us
  Pallas kernels  32.4 us (100%)
    pallas_call x1, Pallas kernels, on_device(): pl.pallas_call(kernel, out_shape=jax.ShapeDtypeStruct((BATCHES, VEL, BLOC...  30.5 us
    pallas_call x1, Pallas kernels, on_device(): pl.pallas_call(place, out_shape=jax.ShapeDtypeStruct((2 * GX, 2 * Q), f32...  1.85 us

profile of v3, /device:TPU:1, one launch (start us, length us, event | category | flops | bytes accessed | tf_op | source)
XLA Modules:
  0.0 32.4 jit_solution(332879781346136468)
XLA Ops:
  0.0 30.5 %step.1.back = f32[2,16,4,1024]{3,2,1,0:T(4,128)} custom-call(f32[64,2048]{1,0:T(8,128)} %refs_0_.1, f32[5,32768]{1,0:T(8,128)} %refs_1_.1, bf16[1024,1280]{1,0:T(8,128)(2,1)} %constant.19.clone.refs_2_, bf16[4,512,512]{2,1,0:T(8,128)(2,1)} %constant.16.clone.refs_3_, bf16[8,256,256]{2,1,0:T(8,128)(2,1)} %constant.17.clone.refs_4_, ...), custom_call_target="tpu_custom_call" | custom-call | tf_op jit(solution)/shard_map/step/pallas_call | solution.py:588
  30.5 1.8 %place.1 = f32[64,2048]{1,0:T(8,128)} custom-call(f32[2,16,4,1024]{3,2,1,0:T(4,128)} %step.1.back), custom_call_target="tpu_custom_call" | custom-call | tf_op jit(solution)/shard_map/place/pallas_call | solution.py:627

commit v4 on v2

--- a/solution.py
+++ b/solution.py
@@ -350,7 +350,8 @@
 
         return carry
 
-    lax.fori_loop(0, chunks, second_phase, 0)
+    for t in range(chunks):
+        second_phase(t, 0)
     keep = pltpu.make_async_copy(send.at[:, vel], recv.at[:, vel], keep_sem.at[0])
     keep.start()
 

time: 32.5 us -> 32.5 us (level)
  no operation moved by 1% of the time
where the time goes in v4:
time: 32.5 us; the launch traced here: 32.4 us
  Pallas kernels  32.4 us (100%)
    pallas_call x1, Pallas kernels, on_device(): pl.pallas_call(kernel, out_shape=jax.ShapeDtypeStruct((BATCHES, VEL, BLOC...  30.5 us
    pallas_call x1, Pallas kernels, on_device(): pl.pallas_call(place, out_shape=jax.ShapeDtypeStruct((2 * GX, 2 * Q), f32...  1.85 us

profile of v4, /device:TPU:1, one launch (start us, length us, event | category | flops | bytes accessed | tf_op | source)
XLA Modules:
  0.0 32.4 jit_solution(7470366820391237722)
XLA Ops:
  0.0 30.5 %step.1.back = f32[2,16,4,1024]{3,2,1,0:T(4,128)} custom-call(f32[64,2048]{1,0:T(8,128)} %refs_0_.1, f32[5,32768]{1,0:T(8,128)} %refs_1_.1, bf16[1024,1280]{1,0:T(8,128)(2,1)} %constant.16.clone.refs_2_, bf16[8,512,512]{2,1,0:T(8,128)(2,1)} %constant.14.clone.refs_3_, bf16[3,256,256]{2,1,0:T(8,128)(2,1)} %constant.15.clone.refs_4_, ...), custom_call_target="tpu_custom_call" | custom-call | tf_op jit(solution)/shard_map/step/pallas_call | solution.py:566
  30.5 1.8 %place.1 = f32[64,2048]{1,0:T(8,128)} custom-call(f32[2,16,4,1024]{3,2,1,0:T(4,128)} %step.1.back), custom_call_target="tpu_custom_call" | custom-call | tf_op jit(solution)/shard_map/place/pallas_call | solution.py:605
